TPU v7x, 32 devices: a whole 2x2x4 slice. The times are simulated.
32 devices in a mesh: snap: 4 (over y, core), gx: 4 (over z), gy: 2 (over x).
Axes of the slice: x: 2, y: 2, z: 4, core: 2. Of those that a mesh axis runs over, the one named last changes fastest.
Arguments:
- displacements: float32 [64, 3, 16, 256], P('snap', None, 'gx', 'gy')
- forces: float32 [64, 3, 16, 256], P('snap', None, 'gx', 'gy')
- neighbours: int32 [8, 16, 256], P(None, 'gx', 'gy'), may hold values 0 or 1
- species: int32 [16, 256], P('gx', 'gy'), may hold values from 0 to 2
- block_of: int32 [16, 256], P('gx', 'gy'), may hold values from 0 to 3, as said below
- precond: float32 [32, 3, 24, 24], P(('gx', 'gy')), may hold values from -0.1 to 0.8, as said below
- vectors: float32 [256, 3, 16, 256], P('snap', None, 'gx', 'gy'), may hold values from -6 to 6
Outputs:
- constants: float32 [32, 3, 24, 3], P(('gx', 'gy'))
- chebyshev: float32 [256, 3, 16, 256], P('snap', None, 'gx', 'gy')
Inputs may be any that keep to these rules, and one draw needn't show every extreme that they name: `block_of`: on each device's 4 x 128 atoms, every block index holds exactly 128 atoms. `precond`: each matrix has its diagonal between 0.4 and 0.8 and small off-diagonal entries.
All inputs are finite; a program needn't handle non-finite values. No bound on the sum of `neighbours` on one device may be relied on, other than what follows from the above.
Results may differ from a plain program's by a relative error of at most 0.00011.
Values sent between devices are 32-bit elements; how exact they have to be, the bound alone decides.
A program may use at most 64 MiB of HBM per device.

v0:
```python
import jax
import jax.numpy as jnp
from jax import lax
from jax.sharding import PartitionSpec as P

AB = 128
NSPEC = 3


offsets = ((-1, -1), (-1, 0), (-1, 1), (0, -1), (0, 1), (1, -1), (1, 0), (1, 1))


def padded_2(cells, sides, width):
    for axis, dim in sides:
        count = lax.axis_size(axis)
        head = lax.slice_in_dim(cells, 0, width, axis=dim)
        tail = lax.slice_in_dim(cells, cells.shape[dim] - width, cells.shape[dim], axis=dim)
        cells = jnp.concatenate(
            [
                lax.ppermute(tail, axis, [(i, (i + 1) % count) for i in range(count)]),
                cells,
                lax.ppermute(head, axis, [((i + 1) % count, i) for i in range(count)]),
            ],
            axis=dim,
        )
    return cells


def apply_operator(extended, weights, rows, cols):
    center = extended[:, :, 1 : 1 + rows, 1 : 1 + cols]
    result = jnp.zeros_like(center)
    for index, (step_x, step_y) in enumerate(offsets):
        moved = extended[:, :, 1 + step_x : 1 + step_x + rows, 1 + step_y : 1 + step_y + cols]
        differ = moved - center
        result = result - jnp.sum(differ[:, :, None] * weights[index][None], axis=1)
    return result


def refine(precond, gram, rhs):
    high = lax.Precision.HIGHEST
    first = jnp.einsum("gpq,gqa->gpa", precond, rhs, precision=high)
    remain = rhs - jnp.einsum("gpq,gqa->gpa", gram, first, precision=high)
    return first + jnp.einsum("gpq,gqa->gpa", precond, remain, precision=high)


def shards(displacements, forces, neighbours, species, block_of, precond, vectors):
    high = lax.Precision.HIGHEST
    snap_dev, _, rows, cols = displacements.shape
    count = rows * cols
    width = 3 * len(offsets)
    padded = padded_2(displacements, (("gx", 2), ("gy", 3)), 1)
    mask = neighbours.astype(jnp.float32)
    parts = []
    for index, (step_x, step_y) in enumerate(offsets):
        moved = padded[:, :, 1 + step_x : 1 + step_x + rows, 1 + step_y : 1 + step_y + cols]
        parts.append((moved - displacements) * mask[index][None, None])
    feats = jnp.stack(parts, 1).reshape(snap_dev, width, count)
    loads = forces.reshape(snap_dev, 3, count)
    n_groups = precond.shape[0] * precond.shape[1]
    group = (block_of * NSPEC + species).reshape(count)
    onehot = (jnp.arange(n_groups, dtype=jnp.int32)[:, None] == group[None, :]).astype(jnp.float32)
    pair = jnp.einsum("spi,sqi->pqi", feats, feats, precision=high).reshape(width * width, count)
    cross = jnp.einsum("spi,sai->pai", feats, loads, precision=high).reshape(width * 3, count)
    gram_part = jnp.dot(pair, onehot.T, precision=high).T.reshape(n_groups, width, width)
    rhs_part = jnp.dot(cross, onehot.T, precision=high).T.reshape(n_groups, width, 3)
    scale = 1.0 / (snap_dev * lax.axis_size("snap") * AB)
    inverses = precond.reshape(n_groups, width, width)
    gram_total, rhs_total = lax.psum((gram_part, rhs_part), "snap")
    theta = refine(inverses, gram_total * scale, rhs_total * scale)
    flat_weights = jnp.dot(theta.reshape(n_groups, width * 3).T, onehot, precision=high)
    flat_weights = flat_weights.reshape(len(offsets), 9, rows, cols) * mask[:, None]
    weights = flat_weights.reshape(len(offsets), 3, 3, rows, cols)

    def with_rim(field):
        return padded_2(field, (("gx", 2), ("gy", 3)), 1)

    first_term = apply_operator(with_rim(vectors), weights, rows, cols)
    chebyshev = 2.0 * apply_operator(with_rim(first_term), weights, rows, cols) - vectors
    return (theta.reshape(precond.shape[0], precond.shape[1], width, 3), chebyshev)


def solution(mesh):
    in_specs = (
        P("snap", None, "gx", "gy"),
        P("snap", None, "gx", "gy"),
        P(None, "gx", "gy"),
        P("gx", "gy"),
        P("gx", "gy"),
        P(("gx", "gy"), None, None, None),
        P("snap", None, "gx", "gy"),
    )
    out_specs = (P(("gx", "gy"), None, None, None), P("snap", None, "gx", "gy"))
    return jax.shard_map(shards, mesh=mesh, in_specs=in_specs, out_specs=out_specs, check_vma=False)
```

profile of v0, /device:TPU:0, one launch (start us, length us, event | category | flops | bytes accessed | tf_op | source)
XLA Modules:
  0.0 98.2 jit_solution(13597817958634177871)
XLA Ops:
  0.7 1.0 %fusion.66 = (f32[16,3,1,128]{3,2,1,0:T(1,128)S(1)}, f32[16,3,1,128]{3,2,1,0:T(1,128)S(1)}) fusion(f32[16,3,4,128]{3,2,1,0:T(4,128)} %param.7), kind=kLoop, calls=%fused_computation.138 | loop fusion | bytes 98304 | tf_op jit(solution)/shard_map/slice | solution.py:17
  1.7 5.1 %collective-permute-start.1 = (f32[16,3,1,128]{3,2,1,0:T(1,128)S(1)}, f32[16,3,1,128]{3,2,1,0:T(1,128)S(1)}, u32[]{:S(2)}, u32[]{:S(2)}) collective-permute-start(f32[16,3,1,128]{3,2,1,0:T(1,128)S(1)} %get-tuple-element.59), channel_id=1, source_target_pairs={{2,0},{4,2},{6,4},{0,6},{3,1},{5,3},{7,5},{1,7},{10,8},{12,10},{14... | collective-permute-start | bytes 73736 | tf_op jit(solution)/shard_map/ppermute | solution.py:22
  6.8 1.3 %fusion.63 = (f32[64,3,1,128]{3,2,1,0:T(1,128)S(1)}, f32[64,3,1,128]{3,2,1,0:T(1,128)S(1)}) fusion(f32[64,3,4,128]{3,2,1,0:T(4,128)} %param.13), kind=kLoop, calls=%fused_computation.135 | loop fusion | bytes 393216 | tf_op jit(solution)/shard_map/slice | solution.py:16
  8.2 3.9 %collective-permute-start.5 = (f32[64,3,1,128]{3,0,2,1:T(8,128)S(1)}, f32[64,3,1,128]{3,0,2,1:T(8,128)S(1)}, u32[]{:S(2)}, u32[]{:S(2)}) collective-permute-start(f32[64,3,1,128]{3,0,2,1:T(8,128)S(1)} %copy.276), channel_id=1, source_target_pairs={{2,0},{4,2},{6,4},{0,6},{3,1},{5,3},{7,5},{1,7},{10,8},{12,10},{14... | collective-permute-start | bytes 294920 | tf_op jit(solution)/shard_map/ppermute | solution.py:22
  12.8 0.7 add_bitcast_fusion
  13.5 1.0 pad_maximum_fusion.8
  14.6 1.6 %collective-permute-start.2 = (f32[16,3,6,1]{3,2,1,0:T(8,128)S(1)}, f32[16,3,6,1]{3,2,1,0:T(8,128)S(1)}, u32[]{:S(2)}, u32[]{:S(2)}) collective-permute-start(f32[16,3,6,1]{3,2,1,0:T(8,128)S(1)} %get-tuple-element.57), channel_id=1, source_target_pairs={{0,1},{1,0},{2,3},{3,2},{4,5},{5,4},{6,7},{7,6},{8,9},{9,8},{10,11... | collective-permute-start | bytes 3464 | tf_op jit(solution)/shard_map/ppermute | solution.py:20
  17.2 5.3 %collective-permute-done.2 = f32[16,3,6,1]{3,2,1,0:T(8,128)S(1)} collective-permute-done((f32[16,3,6,1]{3,2,1,0:T(8,128)S(1)}, f32[16,3,6,1]{3,2,1,0:T(8,128)S(1)}, u32[]{:S(2)}, u32[]{:S(2)}) %collective-permute-start.2) | collective-permute-done | bytes 1184 | tf_op jit(solution)/shard_map/ppermute | solution.py:20
  22.8 1.9 %collective-permute-done.3 = f32[16,3,6,1]{3,2,1,0:T(8,128)S(1)} collective-permute-done((f32[16,3,6,1]{3,2,1,0:T(8,128)S(1)}, f32[16,3,6,1]{3,2,1,0:T(8,128)S(1)}, u32[]{:S(2)}, u32[]{:S(2)}) %collective-permute-start.3) | collective-permute-done | bytes 1184 | tf_op jit(solution)/shard_map/ppermute | solution.py:22
  26.8 3.9 %copy.203 = f32[16,24,512]{1,0,2:T(8,128)} copy(f32[16,24,512]{2,1,0:T(8,128)S(1)} %reshape.100) | data formatting | bytes 1572864 | tf_op jit(solution)/shard_map/reshape | solution.py:57
  30.7 16.9 %convolution_bitcast_fusion = f32[24,24,512]{0,1,2:T(8,128)} fusion(f32[16,24,512]{1,0,2:T(8,128)} %copy.203), kind=kOutput, calls=%fused_computation | convolution fusion | flops 56623104 | bytes 1966080 | tf_op jit(solution)/shard_map/spi,sqi->pqi/dot_general | solution.py:62
  47.6 4.0 %convolution_bitcast_fusion.1 = f32[24,3,512]{0,1,2:T(4,128)S(1)} fusion(f32[16,24,512]{1,0,2:T(8,128)S(1)} %copy-done.1, f32[16,3,512]{0,1,2:T(4,128)S(1)} %bitcast.92), kind=kOutput, calls=%fused_computation.9 | convolution fusion | flops 7077888 | bytes 1032192 | tf_op jit(solution)/shard_map/spi,sai->pai/dot_general | solution.py:63
  52.0 4.7 %copy.209 = f32[24,24,512]{2,1,0:T(8,128)S(1)} copy(f32[24,24,512]{0,1,2:T(8,128)} %convolution_bitcast_fusion) | data formatting | bytes 2359296 | tf_op jit(solution)/shard_map/spi,sqi->pqi/transpose | solution.py:62
  56.7 1.5 %fusion.49 = f32[12,24,24]{2,0,1:T(8,128)S(1)} fusion(f32[24,24,512]{2,1,0:T(8,128)S(1)} %copy.209, s32[512]{0:T(512)S(1)} %add_bitcast_fusion), kind=kOutput, calls=%fused_computation.109 | convolution fusion | flops 42473472 | bytes 1209344 | tf_op jit(solution)/shard_map/dot_general | solution.py:64
  58.3 12.1 %all-reduce = (f32[12,24,3]{1,0,2:T(8,128)S(1)}, f32[12,24,24]{2,1,0:T(8,128)S(1)}) all-reduce(f32[12,24,3]{1,0,2:T(8,128)S(1)} %fusion, f32[12,24,24]{2,1,0:T(8,128)S(1)} %copy.210), channel_id=1, replica_groups=mesh['snap'=4,'gx'=4,'gy'=2] {'snap'}, use_global_device_ids=true, to_apply=%region_0.0 | all-reduce | flops 7776 | bytes 62208 | tf_op jit(solution)/shard_map/psum | solution.py:68
  72.8 1.5 %collective-permute-start.6 = (f32[64,3,6,1]{0,2,3,1:T(8,128)S(1)}, f32[64,3,6,1]{0,2,3,1:T(8,128)S(1)}, u32[]{:S(2)}, u32[]{:S(2)}) collective-permute-start(f32[64,3,6,1]{0,2,3,1:T(8,128)S(1)} %copy.216), channel_id=1, source_target_pairs={{0,1},{1,0},{2,3},{3,2},{4,5},{5,4},{6,7},{7,6},{8,9},{9,8},{10,11... | collective-permute-start | bytes 13832 | tf_op jit(solution)/shard_map/ppermute | solution.py:20
  76.8 1.5 %collective-permute-done.7 = f32[64,3,6,1]{0,2,3,1:T(8,128)S(1)} collective-permute-done((f32[64,3,6,1]{0,2,3,1:T(8,128)S(1)}, f32[64,3,6,1]{0,2,3,1:T(8,128)S(1)}, u32[]{:S(2)}, u32[]{:S(2)}) %collective-permute-start.7) | collective-permute-done | bytes 4640 | tf_op jit(solution)/shard_map/ppermute | solution.py:22
  78.6 1.0 %fusion.9 = (f32[64,3,4,128]{3,0,2,1:T(8,128)S(1)}, f32[64,3,4,128]{3,0,2,1:T(8,128)S(1)}, f32[64,3,4,128]{3,0,2,1:T(8,128)S(1)}, f32[64,3,4,128]{3,0,2,1:T(8,12...) fusion(f32[64,3,6,1]{3,0,2,1:T(8,128)S(1)} %copy.217, ...), kind=kLoop, calls=%fused_computation.40 | loop fusion | flops 1179648 | bytes 3351552 | tf_op jit(solution)/shard_map/sub | solution.py:34
  80.7 1.8 %collective-permute-start.9 = (f32[64,3,1,128]{3,0,2,1:T(8,128)S(1)}, f32[64,3,1,128]{3,0,2,1:T(8,128)S(1)}, u32[]{:S(2)}, u32[]{:S(2)}) collective-permute-start(f32[64,3,1,128]{3,0,2,1:T(8,128)S(1)} %get-tuple-element.43), channel_id=1, source_target_pairs={{2,0},{4,2},{6,4},{0,6},{3,1},{5,3},{7,5},{1,7},{10,8},{12,10},{14... | collective-permute-start | bytes 294920 | tf_op jit(solution)/shard_map/ppermute | solution.py:22
  82.7 2.6 %collective-permute-done.9 = f32[64,3,1,128]{3,0,2,1:T(8,128)S(1)} collective-permute-done((f32[64,3,1,128]{3,0,2,1:T(8,128)S(1)}, f32[64,3,1,128]{3,0,2,1:T(8,128)S(1)}, u32[]{:S(2)}, u32[]{:S(2)}) %collective-permute-start.9) | collective-permute-done | bytes 98336 | tf_op jit(solution)/shard_map/ppermute | solution.py:22
  85.3 3.5 %collective-permute-done.8 = f32[64,3,1,128]{3,0,2,1:T(8,128)S(1)} collective-permute-done((f32[64,3,1,128]{3,0,2,1:T(8,128)S(1)}, f32[64,3,1,128]{3,0,2,1:T(8,128)S(1)}, u32[]{:S(2)}, u32[]{:S(2)}) %collective-permute-start.8) | collective-permute-done | bytes 98336 | tf_op jit(solution)/shard_map/ppermute | solution.py:20
  90.3 1.5 %collective-permute-start.11 = (f32[64,3,6,1]{0,2,3,1:T(8,128)S(1)}, f32[64,3,6,1]{0,2,3,1:T(8,128)S(1)}, u32[]{:S(2)}, u32[]{:S(2)}) collective-permute-start(f32[64,3,6,1]{0,2,3,1:T(8,128)S(1)} %copy.255), channel_id=1, source_target_pairs={{1,0},{0,1},{3,2},{2,3},{5,4},{4,5},{7,6},{6,7},{9,8},{8,9},{11,10... | collective-permute-start | bytes 13832 | tf_op jit(solution)/shard_map/ppermute | solution.py:22
  92.4 0.7 collective-permute-done.10
  97.2 1.0 %copy.248 = f32[64,3,4,128]{3,2,1,0:T(4,128)} copy(f32[64,3,4,128]{3,0,2,1:T(8,128)S(1)} %multiply_subtract_fusion) | data formatting | bytes 786432
  (121 shorter events, 16.9 us)
Async XLA Ops:
  0.6 69.8 %copy-start = (f32[4,3,24,24]{3,2,1,0:T(8,128)S(1)}, f32[4,3,24,24]{3,2,1,0:T(8,128)}, u32[]{:S(2)}) copy-start(f32[4,3,24,24]{3,2,1,0:T(8,128)} %param.12) | copy-start | bytes 82948
  0.6 15.5 %copy-start.16 = (f32[16,3,4,128]{3,2,1,0:T(4,128)S(1)}, f32[16,3,4,128]{3,2,1,0:T(4,128)}, u32[]{:S(2)}) copy-start(f32[16,3,4,128]{3,2,1,0:T(4,128)} %param.8) | copy-start | bytes 294916
  1.7 11.8 %collective-permute-start.1 = (f32[16,3,1,128]{3,2,1,0:T(1,128)S(1)}, f32[16,3,1,128]{3,2,1,0:T(1,128)S(1)}, u32[]{:S(2)}, u32[]{:S(2)}) collective-permute-start(f32[16,3,1,128]{3,2,1,0:T(1,128)S(1)} %get-tuple-element.59), channel_id=1, source_target_pairs={{2,0},{4,2},{6,4},{0,6},{3,1},{5,3},{7,5},{1,7},{10,8},{12,10},{14... | collective-permute-start | bytes 73736 | tf_op jit(solution)/shard_map/ppermute | solution.py:22
  6.8 6.7 %collective-permute-start = (f32[16,3,1,128]{3,2,1,0:T(1,128)S(1)}, f32[16,3,1,128]{3,2,1,0:T(1,128)S(1)}, u32[]{:S(2)}, u32[]{:S(2)}) collective-permute-start(f32[16,3,1,128]{3,2,1,0:T(1,128)S(1)} %get-tuple-element.58), channel_id=1, source_target_pairs={{0,2},{2,4},{4,6},{6,0},{1,3},{3,5},{5,7},{7,1},{8,10},{10,12},{12... | collective-permute-start | bytes 73736 | tf_op jit(solution)/shard_map/ppermute | solution.py:20
  8.1 64.1 %collective-permute-start.4 = (f32[64,3,1,128]{3,0,2,1:T(8,128)S(1)}, f32[64,3,1,128]{3,0,2,1:T(8,128)S(1)}, u32[]{:S(2)}, u32[]{:S(2)}) collective-permute-start(f32[64,3,1,128]{3,0,2,1:T(8,128)S(1)} %copy.275), channel_id=1, source_target_pairs={{0,2},{2,4},{4,6},{6,0},{1,3},{3,5},{5,7},{7,1},{8,10},{10,12},{12... | collective-permute-start | bytes 294920 | tf_op jit(solution)/shard_map/ppermute | solution.py:20
  8.2 64.1 %collective-permute-start.5 = (f32[64,3,1,128]{3,0,2,1:T(8,128)S(1)}, f32[64,3,1,128]{3,0,2,1:T(8,128)S(1)}, u32[]{:S(2)}, u32[]{:S(2)}) collective-permute-start(f32[64,3,1,128]{3,0,2,1:T(8,128)S(1)} %copy.276), channel_id=1, source_target_pairs={{2,0},{4,2},{6,4},{0,6},{3,1},{5,3},{7,5},{1,7},{10,8},{12,10},{14... | collective-permute-start | bytes 294920 | tf_op jit(solution)/shard_map/ppermute | solution.py:22
  12.8 9.7 %copy-start.2 = (f32[16,3,4,128]{3,2,1,0:T(4,128)S(1)}, f32[16,3,4,128]{3,2,1,0:T(4,128)}, u32[]{:S(2)}) copy-start(f32[16,3,4,128]{3,2,1,0:T(4,128)} %param.7) | copy-start | bytes 294916
  14.6 7.9 %collective-permute-start.2 = (f32[16,3,6,1]{3,2,1,0:T(8,128)S(1)}, f32[16,3,6,1]{3,2,1,0:T(8,128)S(1)}, u32[]{:S(2)}, u32[]{:S(2)}) collective-permute-start(f32[16,3,6,1]{3,2,1,0:T(8,128)S(1)} %get-tuple-element.57), channel_id=1, source_target_pairs={{0,1},{1,0},{2,3},{3,2},{4,5},{5,4},{6,7},{7,6},{8,9},{9,8},{10,11... | collective-permute-start | bytes 3464 | tf_op jit(solution)/shard_map/ppermute | solution.py:20
  16.6 8.1 %collective-permute-start.3 = (f32[16,3,6,1]{3,2,1,0:T(8,128)S(1)}, f32[16,3,6,1]{3,2,1,0:T(8,128)S(1)}, u32[]{:S(2)}, u32[]{:S(2)}) collective-permute-start(f32[16,3,6,1]{3,2,1,0:T(8,128)S(1)} %get-tuple-element.56), channel_id=1, source_target_pairs={{1,0},{0,1},{3,2},{2,3},{5,4},{4,5},{7,6},{6,7},{9,8},{8,9},{11,10... | collective-permute-start | bytes 3464 | tf_op jit(solution)/shard_map/ppermute | solution.py:22
  30.7 16.9 %copy-start.1 = (f32[16,24,512]{1,0,2:T(8,128)S(1)}, f32[16,24,512]{1,0,2:T(8,128)}, u32[]{:S(2)}) copy-start(f32[16,24,512]{1,0,2:T(8,128)} %copy.203) | copy-start | bytes 2359300
  70.5 1.7 %copy-start.3 = (f32[64,3,4,128]{3,2,1,0:T(4,128)S(1)}, f32[64,3,4,128]{3,2,1,0:T(4,128)}, u32[]{:S(2)}) copy-start(f32[64,3,4,128]{3,2,1,0:T(4,128)} %param.13) | copy-start | bytes 1179652
  72.0 7.6 %copy-start.12 = (f32[1,9,4,128]{3,2,1,0:T(4,128)}, f32[1,9,4,128]{3,2,1,0:T(4,128)S(1)}, u32[]{:S(2)}) copy-start(f32[1,9,4,128]{3,2,1,0:T(4,128)S(1)} %copy.241) | copy-start | bytes 55300
  72.0 7.6 %copy-start.4 = (f32[1,9,4,128]{3,2,1,0:T(4,128)}, f32[1,9,4,128]{3,2,1,0:T(4,128)S(1)}, u32[]{:S(2)}) copy-start(f32[1,9,4,128]{3,2,1,0:T(4,128)S(1)} %copy.236) | copy-start | bytes 55300
  72.1 3.8 %copy-start.14 = (f32[1,9,4,128]{3,2,1,0:T(4,128)}, f32[1,9,4,128]{3,2,1,0:T(4,128)S(1)}, u32[]{:S(2)}) copy-start(f32[1,9,4,128]{3,2,1,0:T(4,128)S(1)} %copy.239) | copy-start | bytes 55300
  72.1 7.7 %copy-start.10 = (f32[1,9,4,128]{3,2,1,0:T(4,128)}, f32[1,9,4,128]{3,2,1,0:T(4,128)S(1)}, u32[]{:S(2)}) copy-start(f32[1,9,4,128]{3,2,1,0:T(4,128)S(1)} %copy.234) | copy-start | bytes 55300
  72.1 7.7 %copy-start.8 = (f32[1,9,4,128]{3,2,1,0:T(4,128)}, f32[1,9,4,128]{3,2,1,0:T(4,128)S(1)}, u32[]{:S(2)}) copy-start(f32[1,9,4,128]{3,2,1,0:T(4,128)S(1)} %copy.232) | copy-start | bytes 55300
  72.2 7.9 %copy-start.6 = (f32[1,9,4,128]{3,2,1,0:T(4,128)}, f32[1,9,4,128]{3,2,1,0:T(4,128)S(1)}, u32[]{:S(2)}) copy-start(f32[1,9,4,128]{3,2,1,0:T(4,128)S(1)} %copy.230) | copy-start | bytes 55300
  72.8 3.7 %collective-permute-start.6 = (f32[64,3,6,1]{0,2,3,1:T(8,128)S(1)}, f32[64,3,6,1]{0,2,3,1:T(8,128)S(1)}, u32[]{:S(2)}, u32[]{:S(2)}) collective-permute-start(f32[64,3,6,1]{0,2,3,1:T(8,128)S(1)} %copy.216), channel_id=1, source_target_pairs={{0,1},{1,0},{2,3},{3,2},{4,5},{5,4},{6,7},{7,6},{8,9},{9,8},{10,11... | collective-permute-start | bytes 13832 | tf_op jit(solution)/shard_map/ppermute | solution.py:20
  74.6 3.7 %collective-permute-start.7 = (f32[64,3,6,1]{0,2,3,1:T(8,128)S(1)}, f32[64,3,6,1]{0,2,3,1:T(8,128)S(1)}, u32[]{:S(2)}, u32[]{:S(2)}) collective-permute-start(f32[64,3,6,1]{0,2,3,1:T(8,128)S(1)} %copy.227), channel_id=1, source_target_pairs={{1,0},{0,1},{3,2},{2,3},{5,4},{4,5},{7,6},{6,7},{9,8},{8,9},{11,10... | collective-permute-start | bytes 13832 | tf_op jit(solution)/shard_map/ppermute | solution.py:22
  80.7 4.7 %collective-permute-start.9 = (f32[64,3,1,128]{3,0,2,1:T(8,128)S(1)}, f32[64,3,1,128]{3,0,2,1:T(8,128)S(1)}, u32[]{:S(2)}, u32[]{:S(2)}) collective-permute-start(f32[64,3,1,128]{3,0,2,1:T(8,128)S(1)} %get-tuple-element.43), channel_id=1, source_target_pairs={{2,0},{4,2},{6,4},{0,6},{3,1},{5,3},{7,5},{1,7},{10,8},{12,10},{14... | collective-permute-start | bytes 294920 | tf_op jit(solution)/shard_map/ppermute | solution.py:22
  82.4 6.4 %collective-permute-start.8 = (f32[64,3,1,128]{3,0,2,1:T(8,128)S(1)}, f32[64,3,1,128]{3,0,2,1:T(8,128)S(1)}, u32[]{:S(2)}, u32[]{:S(2)}) collective-permute-start(f32[64,3,1,128]{3,0,2,1:T(8,128)S(1)} %get-tuple-element.42), channel_id=1, source_target_pairs={{0,2},{2,4},{4,6},{6,0},{1,3},{3,5},{5,7},{7,1},{8,10},{10,12},{12... | collective-permute-start | bytes 294920 | tf_op jit(solution)/shard_map/ppermute | solution.py:20
  89.4 3.7 %collective-permute-start.10 = (f32[64,3,6,1]{0,2,3,1:T(8,128)S(1)}, f32[64,3,6,1]{0,2,3,1:T(8,128)S(1)}, u32[]{:S(2)}, u32[]{:S(2)}) collective-permute-start(f32[64,3,6,1]{0,2,3,1:T(8,128)S(1)} %copy.254), channel_id=1, source_target_pairs={{0,1},{1,0},{2,3},{3,2},{4,5},{5,4},{6,7},{7,6},{8,9},{9,8},{10,11... | collective-permute-start | bytes 13832 | tf_op jit(solution)/shard_map/ppermute | solution.py:20
  90.3 3.7 %collective-permute-start.11 = (f32[64,3,6,1]{0,2,3,1:T(8,128)S(1)}, f32[64,3,6,1]{0,2,3,1:T(8,128)S(1)}, u32[]{:S(2)}, u32[]{:S(2)}) collective-permute-start(f32[64,3,6,1]{0,2,3,1:T(8,128)S(1)} %copy.255), channel_id=1, source_target_pairs={{1,0},{0,1},{3,2},{2,3},{5,4},{4,5},{7,6},{6,7},{9,8},{8,9},{11,10... | collective-permute-start | bytes 13832 | tf_op jit(solution)/shard_map/ppermute | solution.py:22
  94.7 0.8 copy-start.15
  (5 other events, 3.6 us)
where the time goes:
time: 98.7 us; the launch traced here: 98.2 us
  matrix products  24.1 us (24%)
  local copies, waits for them, and re-layouts  17.8 us (18%)
  starting transfers between devices  17.5 us (18%)
  waiting for transfers between devices  16.6 us (17%)
  blocking collectives  12.1 us (12%)
  other arithmetic  8.86 us (9%)
  between operations  1.27 us (1%)
    dot_general x1, matrix products, shards(): jnp.einsum('spi,sqi->pqi', feats, feats, precision=high)  16.9 us
    ppermute x6, starting transfers between devices, padded_2(): lax.ppermute(head, axis, [((i + 1) % count, i) for i in range(count)])  13.5 us
    psum x1, blocking collectives, shards(): gram_total, rhs_total = lax.psum((gram_part, rhs_part), 'snap')  12.1 us
    ppermute x6, waiting for transfers between devices, padded_2(): lax.ppermute(tail, axis, [(i, (i + 1) % count) for i in range(count)])  10 us
    ppermute x6, waiting for transfers between devices, padded_2(): lax.ppermute(head, axis, [((i + 1) % count, i) for i in range(count)])  6.61 us
    transpose x1, local copies, waits for them, and re-layouts, shards(): jnp.einsum('spi,sqi->pqi', feats, feats, precision=high)  4.65 us
    reshape x2, local copies, waits for them, and re-layouts, shards(): feats = jnp.stack(parts, 1).reshape(snap_dev, width, count)  4.23 us
    ppermute x6, starting transfers between devices, padded_2(): lax.ppermute(tail, axis, [(i, (i + 1) % count) for i in range(count)])  4.03 us
  transfers between devices with their start and end apart: 12, of which 8 were waited for; matrix products, arithmetic and copies ran while one was open for 43% of the time, Pallas kernels for 0%

commit v1 on v0

v1 whole, which is shorter than its diff:
```python
import functools

import jax
import jax.numpy as jnp
import numpy as np
from jax import lax
from jax.experimental import pallas as pl
from jax.experimental.pallas import tpu as pltpu
from jax.sharding import PartitionSpec as P

AB = 128
NSPEC = 3
GP = 16
WIDTH = 24
PAIRS = [(p, q) for p in range(WIDTH) for q in range(p, WIDTH)]
NPAIR = len(PAIRS)
ENTRIES = 384
PARTS = 2
MESH = pl.DeviceIdType.MESH

offsets = ((-1, -1), (-1, 0), (-1, 1), (0, -1), (0, 1), (1, -1), (1, 0), (1, 1))


def expansion():
    table = np.zeros((608, ENTRIES), np.float32)
    for index, (p, q) in enumerate(PAIRS):
        table[p * WIDTH + q, index] = 1.0
        table[q * WIDTH + p, index] = 1.0
    for p in range(WIDTH):
        for a in range(3):
            table[WIDTH * WIDTH + p, NPAIR + 3 * p + a] = 1.0
    return table


def split(value, parts):
    out = []
    for _ in range(parts):
        piece = value.astype(jnp.bfloat16)
        out.append(piece)
        value = value - piece.astype(jnp.float32)
    return out


def dot_nt(left, right):
    return lax.dot_general(left, right, (((1,), (1,)), ((), ())), preferred_element_type=jnp.float32)


def dot_nn(left, right):
    return lax.dot_general(left, right, (((1,), (0,)), ((), ())), preferred_element_type=jnp.float32)


def kernel(
    n_snap, n_gx, n_gy, n_dev, v_dev, scale,
    disp, forc, neigh, spec, blk, pre, table, vec,
    theta_out, out,
    ed, ev, ef, pk, pleft, pright, ce, pf, fleft, fright, cf,
    de, ms, prs, tall, ws, wc,
    bar_rows_s, bar_rows_r, pk_s, pk_r, t_s, t_r, f_s, f_r,
):
    me = lax.axis_index("snap")
    gx = lax.axis_index("gx")
    gy = lax.axis_index("gy")
    up = lax.rem(gx + n_gx - 1, n_gx)
    down = lax.rem(gx + 1, n_gx)
    left = lax.rem(gy + n_gy - 1, n_gy)
    right = lax.rem(gy + 1, n_gy)
    sides = (left, right) if n_gy > 2 else (right,)
    peers = [lax.rem(me + k, n_snap) for k in range(1, n_snap)]

    barrier = pltpu.get_barrier_semaphore()
    around = [(x, gy) for x in (up, down)] + [(x, y) for y in sides for x in (up, gx, down)]
    for x, y in around:
        pl.semaphore_signal(barrier, inc=1, device_id=(me, x, y), device_id_type=MESH)
    for peer in peers:
        pl.semaphore_signal(barrier, inc=1, device_id=(peer, gx, gy), device_id_type=MESH)

    lane = lax.broadcasted_iota(jnp.int32, (8, 128), 1)
    first_lane = lane == 0
    last_lane = lane == 127
    even = lane % 2 == 0
    v_chunks = v_dev // 8
    d_chunks = n_dev // 8

    def pack_into(current, value, index):
        place = 2 * index
        return jnp.where((lane == place) | (lane == place + 1), pltpu.roll(value, place + 1, 1), current)

    def row_copies(field, at, send, recv):
        return [
            pltpu.make_async_remote_copy(
                src_ref=field.at[pl.ds(source, 3), at], dst_ref=field.at[pl.ds(target, 3), at],
                send_sem=send.at[k], recv_sem=recv.at[k], device_id=(me, x, gy), device_id_type=MESH)
            for k, (source, target, x) in enumerate(((12, 0, down), (3, 15, up)))
        ]

    def column_copies(packed, to_left, to_right, send, recv, first):
        made = []
        for side, (y, target) in enumerate(((right, to_left), (left, to_right))):
            for k, (source, place, size, x) in enumerate(((0, 3, 12, gx), (9, 0, 3, down), (0, 15, 3, up))):
                number = first + side * 3 + k
                made.append(pltpu.make_async_remote_copy(
                    src_ref=packed.at[pl.ds(source, size)], dst_ref=target.at[pl.ds(place, size)],
                    send_sem=send.at[number], recv_sem=recv.at[number], device_id=(me, x, y), device_id_type=MESH))
        return made

    def join_columns(from_left, from_right, target):
        for row in range(18):
            target[row] = jnp.where(even, pltpu.roll(from_right[row], 127, 1), pltpu.roll(from_left[row], 1, 1))

    for x in range(4):
        for b in range(3):
            row = x * 3 + b
            packed = jnp.zeros((8, 128), jnp.float32)
            for c in range(d_chunks):
                value = disp[pl.ds(c * 96 + b * 4 + x, 8, stride=12), :]
                ed[row + 3, pl.ds(c * 8, 8), :] = value
                packed = pack_into(packed, value, v_chunks + c)
            for c in range(v_chunks):
                value = vec[pl.ds(c * 96 + b * 4 + x, 8, stride=12), :]
                ev[row + 3, pl.ds(c * 8, 8), :] = value
                packed = pack_into(packed, value, c)
            pk[row] = packed

    pl.semaphore_wait(barrier, len(around) + len(peers))
    d_rows = row_copies(ed, pl.ds(0, n_dev), bar_rows_s.at[0], bar_rows_r.at[0])
    cols = column_copies(pk, pleft, pright, pk_s, pk_r, 0)
    v_rows = row_copies(ev, pl.ds(0, v_dev), bar_rows_s.at[1], bar_rows_r.at[1])
    for copy in d_rows + cols + v_rows:
        copy.start()

    for o in range(8):
        for x in range(4):
            mask = neigh[pl.ds(o * 4 + x, 1), :].astype(jnp.float32)
            for b in range(3):
                ms[x, pl.ds(3 * o + b, 1), :] = mask
    prs[pl.ds(372 * 8, 12 * 8), :] = jnp.zeros((12 * 8, 128), jnp.float32)
    group = blk[...] * NSPEC + spec[...]
    sub = lax.broadcasted_iota(jnp.int32, (GP * 3, 128), 0) % GP

    for copy in d_rows + cols:
        copy.wait_recv()
    join_columns(pleft, pright, ce)

    for row in range(18):
        for c in range(d_chunks):
            value = ed[row, pl.ds(c * 8, 8), :]
            rim = pltpu.roll(ce[row], 128 - (2 * (v_chunks + c) + 1), 1)
            de[0, row, pl.ds(c * 8, 8), :] = jnp.where(first_lane, rim, pltpu.roll(value, 1, 1))
            de[1, row, pl.ds(c * 8, 8), :] = value
            de[2, row, pl.ds(c * 8, 8), :] = jnp.where(last_lane, rim, pltpu.roll(value, 127, 1))

    total = jnp.zeros((GP, ENTRIES), jnp.float32)
    for x in range(4):
        feats = []
        for o, (dx, dy) in enumerate(offsets):
            for b in range(3):
                differ = de[dy + 1, (x + 1 + dx) * 3 + b] - de[1, (x + 1) * 3 + b]
                feats.append(differ * ms[x, pl.ds(3 * o + b, 1), :])
        loads = [forc[pl.ds(a * 4 + x, n_dev, stride=12), :] for a in range(3)]

        def fold(product):
            return sum(product[c * 8:(c + 1) * 8] for c in range(d_chunks))

        for index, (p, q) in enumerate(PAIRS):
            prs[pl.ds(index * 8, 8), :] = fold(feats[p] * feats[q])
        for p in range(WIDTH):
            for a in range(3):
                prs[pl.ds((NPAIR + 3 * p + a) * 8, 8), :] = fold(feats[p] * loads[a])
        summed = prs[pl.ds(0, ENTRIES, stride=8), :]
        for k in range(1, 8):
            summed = summed + prs[pl.ds(k, ENTRIES, stride=8), :]
        hot = (sub[:GP] == group[x:x + 1, :]).astype(jnp.float32).astype(jnp.bfloat16)
        for piece in split(summed, 2):
            total = total + dot_nt(hot, piece)

    tall[me] = total
    t_copies = []
    for k, peer in enumerate(peers):
        copy = pltpu.make_async_remote_copy(
            src_ref=tall.at[me], dst_ref=tall.at[me], send_sem=t_s.at[k], recv_sem=t_r.at[me],
            device_id=(peer, gx, gy), device_id_type=MESH)
        copy.start()
        t_copies.append(copy)
    for k, peer in enumerate(peers):
        pltpu.make_async_remote_copy(
            src_ref=tall.at[me], dst_ref=tall.at[peer], send_sem=t_s.at[k], recv_sem=t_r.at[peer],
            device_id=(peer, gx, gy), device_id_type=MESH).wait_recv()
    total = tall[0]
    for k in range(1, n_snap):
        total = total + tall[k]
    total = total * scale

    wide = jnp.concatenate([total, total, total], axis=0)
    column = lax.broadcasted_iota(jnp.int32, (GP * 3, ENTRIES), 1)
    comp = lax.broadcasted_iota(jnp.int32, (GP * 3, ENTRIES), 0) // GP
    wide = jnp.where((column < NPAIR) | (lax.rem(column, 3) == comp), wide, 0.0)
    full = sum(dot_nt(table[...], piece) for piece in split(wide, 3))
    gram = full[: WIDTH * WIDTH].reshape(WIDTH, WIDTH, GP * 3)
    rhs = full[WIDTH * WIDTH: WIDTH * WIDTH + WIDTH]
    inverse = pre[...].reshape(WIDTH, WIDTH, GP * 3)
    first = jnp.sum(inverse * rhs[None], axis=1)
    remain = rhs - jnp.sum(gram * first[None], axis=1)
    theta = first + jnp.sum(inverse * remain[None], axis=1)
    theta_out[...] = theta

    held = lax.broadcasted_iota(jnp.int32, (WIDTH, GP * 3), 1) // GP
    stacked = jnp.concatenate([jnp.where(held == a, theta, 0.0) for a in range(3)], axis=0)
    pieces = split(stacked, 3)
    for x in range(4):
        hot = (sub == group[x:x + 1, :]).astype(jnp.float32).astype(jnp.bfloat16)
        values = sum(dot_nn(piece, hot) for piece in pieces)
        mask = ms[x]
        ws[x] = values * jnp.concatenate([mask, mask, mask], axis=0)
        for a in range(3):
            for b in range(3):
                wc[x, pl.ds(a * 3 + b, 1), :] = jnp.sum(
                    ws[x, pl.ds(a * WIDTH + b, 8, stride=3), :], axis=0, keepdims=True)

    def stencil(field, rims, chunk, index, emit):
        start = pl.multiple_of(chunk * 8, 8)
        shift = 128 - (2 * index + 1)
        rows = []
        for row in range(18):
            value = field[row, pl.ds(start, 8), :]
            rim = pltpu.roll(rims[row], shift, 1)
            rows.append((
                jnp.where(first_lane, rim, pltpu.roll(value, 1, 1)),
                value,
                jnp.where(last_lane, rim, pltpu.roll(value, 127, 1)),
            ))
        for x in range(4):
            for a in range(3):
                acc = None
                for b in range(3):
                    term = wc[x, pl.ds(a * 3 + b, 1), :] * rows[(x + 1) * 3 + b][1]
                    acc = term if acc is None else acc + term
                for o, (dx, dy) in enumerate(offsets):
                    for b in range(3):
                        acc = acc - ws[x, pl.ds(a * WIDTH + 3 * o + b, 1), :] * rows[(x + 1 + dx) * 3 + b][dy + 1]
                emit(x, a, start, acc)

    for copy in v_rows:
        copy.wait_recv()

    per = v_chunks // PARTS
    f_copies = []
    for part in range(PARTS):
        pf[part] = jnp.zeros((12, 8, 128), jnp.float32)

        def first_step(k, carry, part=part):
            chunk = part * per + k

            def emit(x, a, start, acc):
                row = x * 3 + a
                ef[row + 3, pl.ds(start, 8), :] = acc
                pf[part, row] = pack_into(pf[part, row], acc, k)

            stencil(ev, ce, chunk, chunk, emit)
            return carry

        lax.fori_loop(0, per, first_step, 0)
        rows = row_copies(ef, pl.ds(part * per * 8, per * 8), f_s.at[part], f_r.at[part])
        columns = column_copies(pf.at[part], fleft.at[part], fright.at[part], f_s.at[part], f_r.at[part], 2)
        for copy in columns + rows:
            copy.start()
        f_copies.append(columns + rows)

    for part in range(PARTS):
        for copy in f_copies[part]:
            copy.wait_recv()
        join_columns(fleft.at[part], fright.at[part], cf)

        def second_step(k, carry, part=part):
            chunk = part * per + k

            def emit(x, a, start, acc):
                own = ev[(x + 1) * 3 + a, pl.ds(start, 8), :]
                out[pl.ds(chunk * 96 + a * 4 + x, 8, stride=12), :] = 2.0 * acc - own

            stencil(ef, cf, chunk, k, emit)
            return carry

        lax.fori_loop(0, per, second_step, 0)

    for copy in d_rows + cols + v_rows + t_copies + sum(f_copies, []):
        copy.wait_send()


def shards(displacements, forces, neighbours, species, block_of, precond, vectors):
    n_dev, _, rows, cols = displacements.shape
    v_dev = vectors.shape[0]
    n_snap, n_gx, n_gy = (lax.axis_size(name) for name in ("snap", "gx", "gy"))
    n_groups = precond.shape[0] * precond.shape[1]
    scale = 1.0 / (n_dev * n_snap * AB)
    inverse = precond.reshape(n_groups, WIDTH, WIDTH).transpose(1, 2, 0).reshape(WIDTH * WIDTH, n_groups)
    inverse = jnp.pad(inverse, ((0, 0), (0, GP - n_groups)))
    inverse = jnp.concatenate([inverse] * 3, axis=1)
    table = jnp.asarray(expansion(), jnp.bfloat16)
    vmem = pl.BlockSpec(memory_space=pltpu.VMEM)
    f32 = jnp.float32
    dma = pltpu.SemaphoreType.DMA
    theta, out = pl.pallas_call(
        functools.partial(kernel, n_snap, n_gx, n_gy, n_dev, v_dev, scale),
        out_shape=(
            jax.ShapeDtypeStruct((WIDTH, GP * 3), f32),
            jax.ShapeDtypeStruct((v_dev * 12, cols), f32),
        ),
        in_specs=[vmem] * 8,
        out_specs=(vmem, vmem),
        scratch_shapes=[
            pltpu.VMEM((18, n_dev, cols), f32),
            pltpu.VMEM((18, v_dev, cols), f32),
            pltpu.VMEM((18, v_dev, cols), f32),
            pltpu.VMEM((12, 8, cols), f32),
            pltpu.VMEM((18, 8, cols), f32),
            pltpu.VMEM((18, 8, cols), f32),
            pltpu.VMEM((18, 8, cols), f32),
            pltpu.VMEM((PARTS, 12, 8, cols), f32),
            pltpu.VMEM((PARTS, 18, 8, cols), f32),
            pltpu.VMEM((PARTS, 18, 8, cols), f32),
            pltpu.VMEM((18, 8, cols), f32),
            pltpu.VMEM((3, 18, n_dev, cols), f32),
            pltpu.VMEM((4, WIDTH, cols), f32),
            pltpu.VMEM((ENTRIES * 8, cols), f32),
            pltpu.VMEM((n_snap, GP, ENTRIES), f32),
            pltpu.VMEM((4, 3 * WIDTH, cols), f32),
            pltpu.VMEM((4, 16, cols), f32),
            dma((2, 2)), dma((2, 2)), dma((6,)), dma((6,)),
            dma((n_snap,)), dma((n_snap,)), dma((PARTS, 8)), dma((PARTS, 8)),
        ],
        compiler_params=pltpu.CompilerParams(
            collective_id=0, has_side_effects=True, vmem_limit_bytes=40 * 1024 * 1024),
        name="fit_and_apply",
    )(
        displacements.reshape(n_dev * 12, cols), forces.reshape(n_dev * 12, cols),
        neighbours.reshape(32, cols), species, block_of, inverse, table, vectors.reshape(v_dev * 12, cols),
    )
    theta = theta.reshape(WIDTH, 3, GP)[:, :, :n_groups].transpose(2, 0, 1)
    return (
        theta.reshape(precond.shape[0], precond.shape[1], WIDTH, 3),
        out.reshape(v_dev, 3, rows, cols),
    )


def solution(mesh):
    in_specs = (
        P("snap", None, "gx", "gy"),
        P("snap", None, "gx", "gy"),
        P(None, "gx", "gy"),
        P("gx", "gy"),
        P("gx", "gy"),
        P(("gx", "gy"), None, None, None),
        P("snap", None, "gx", "gy"),
    )
    out_specs = (P(("gx", "gy"), None, None, None), P("snap", None, "gx", "gy"))
    return jax.shard_map(shards, mesh=mesh, in_specs=in_specs, out_specs=out_specs, check_vma=False)
```

time: 98.7 us -> 36.4 us (0.37)
  Pallas kernels: 0 us -> 28.8 us
  matrix products: 24.1 us -> 0 us
  starting transfers between devices: 17.5 us -> 0 us
  waiting for transfers between devices: 16.6 us -> 0 us
  blocking collectives: 12.1 us -> 0 us
  local copies, waits for them, and re-layouts: 17.8 us -> 6.57 us
  other arithmetic: 8.86 us -> 0.01 us
    pallas_call x0 -> x1, Pallas kernels: none -> 28.8 us  [shards(): pl.pallas_call(functools.partial(kernel, n_snap, n_gx, n_gy, n_dev, v_dev...]
    dot_general x8 -> x0, matrix products: 24.1 us -> none  [the longest x1 16.9 us: shards(): jnp.einsum('spi,sqi->pqi', feats, feats, precision=high)]
    ppermute x12 -> x0, starting transfers between devices: 17.5 us -> none  [the longest x6 13.5 us: padded_2(): lax.ppermute(head, axis, [((i + 1) % count, i) for i in range(count)])]
    ppermute x12 -> x0, waiting for transfers between devices: 16.6 us -> none  [the longest x6 10 us: padded_2(): lax.ppermute(tail, axis, [(i, (i + 1) % count) for i in range(count)])]
    psum x1 -> x0, blocking collectives: 12.1 us -> none  [shards(): gram_total, rhs_total = lax.psum((gram_part, rhs_part), 'snap')]
    transpose x1 -> x2, local copies, waits for them, and re-layouts: 4.65 us -> 0.02 us  [shards(): theta = theta.reshape(WIDTH, 3, GP)[:, :, :n_groups].transpose(2, 0, 1)]
    reshape x4 -> x1, local copies, waits for them, and re-layouts: 4.67 us -> 1.09 us  [shards(): precond.reshape(n_groups, WIDTH, WIDTH).transpose(1, 2, 0)]
    slice x17 -> x0, local copies, waits for them, and re-layouts: 3.55 us -> none  [the longest x5 1.78 us: padded_2(): lax.slice_in_dim(cells, cells.shape[dim] - width, cells.shape[dim], axis=...]
  transfers between devices with their start and end apart: 12 -> 0, of which waited for: 8 -> 0; matrix products, arithmetic and copies ran while one was open for 43% -> 0% of each run, Pallas kernels for 0% -> 0%
where the time goes in v1:
time: 36.4 us; the launch traced here: 36.1 us
  Pallas kernels  28.8 us (79%)
  local copies, waits for them, and re-layouts  6.57 us (18%)
  between operations  0.72 us (2%)
    pallas_call x1, Pallas kernels, shards(): pl.pallas_call(functools.partial(kernel, n_snap, n_gx, n_gy, n_dev, v_dev...  28.8 us
    unnamed x16, local copies, waits for them, and re-layouts  5.23 us
    reshape x1, local copies, waits for them, and re-layouts, shards(): precond.reshape(n_groups, WIDTH, WIDTH).transpose(1, 2, 0)  1.09 us

profile of v1, /device:TPU:0, one launch (start us, length us, event | category | flops | bytes accessed | tf_op | source)
XLA Modules:
  0.0 36.1 jit_solution(8153023945521427044)
XLA Ops:
  0.6 0.0 copy-start
  0.6 0.0 copy-start.1
  0.7 1.1 %reshape.35 = f32[576,12]{0,1:T(8,128)S(1)} reshape(f32[24,24,12]{1,0,2:T(8,128)} %bitcast.19) | data formatting | bytes 55296 | tf_op jit(solution)/shard_map/reshape | solution.py:295
  1.8 0.1 copy.15.pre
  1.9 0.0 copy-done
  1.9 0.0 copy-done.1
  2.0 0.0 copy-start.2
  2.0 0.9 %copy-done.2 = f32[16,3,4,128]{3,2,1,0:T(4,128)S(1)} copy-done((f32[16,3,4,128]{3,2,1,0:T(4,128)S(1)}, f32[16,3,4,128]{3,2,1,0:T(4,128)}, u32[]{:S(2)}) %copy-start.2) | copy-done | bytes 98328
  2.8 0.0 copy-start.3
  2.9 0.9 %copy-done.3 = f32[16,3,4,128]{3,2,1,0:T(4,128)S(1)} copy-done((f32[16,3,4,128]{3,2,1,0:T(4,128)S(1)}, f32[16,3,4,128]{3,2,1,0:T(4,128)}, u32[]{:S(2)}) %copy-start.3) | copy-done | bytes 98328
  3.7 0.0 copy-start.4
  3.7 0.7 %copy-done.4 = s32[8,4,128]{2,1,0:T(4,128)S(1)} copy-done((s32[8,4,128]{2,1,0:T(4,128)S(1)}, s32[8,4,128]{2,1,0:T(4,128)}, u32[]{:S(2)}) %copy-start.4) | copy-done | bytes 16408
  4.5 0.0 copy-start.5
  4.5 0.7 %copy-done.5 = s32[4,128]{1,0:T(4,128)S(1)} copy-done((s32[4,128]{1,0:T(4,128)S(1)}, s32[4,128]{1,0:T(4,128)}, u32[]{:S(2)}) %copy-start.5) | copy-done | bytes 2072
  5.1 0.0 copy-start.6
  5.1 0.7 %copy-done.6 = s32[4,128]{1,0:T(4,128)S(1)} copy-done((s32[4,128]{1,0:T(4,128)S(1)}, s32[4,128]{1,0:T(4,128)}, u32[]{:S(2)}) %copy-start.6) | copy-done | bytes 2072
  5.8 28.8 %fit_and_apply.1 = (f32[24,48]{1,0:T(8,128)S(1)}, f32[768,128]{1,0:T(8,128)S(1)}) custom-call(f32[192,128]{1,0:T(8,128)S(1)} %bitcast.16, f32[192,128]{1,0:T(8,128)S(1)} %bitcast.17, s32[32,128]{1,0:T(8,128)S(1)} %bitcast.18, s32[4,128]{1,0:T(4,128)S(1)} %copy-done.5, s32[4,128]{1,0:T(4,128)S(1)} %copy-done.6, f32[576,48]{1,0:T(8,128)S(1)} %copy.15.pre, ...), custom_call_target="tpu_custom_call" | custom-call | tf_op jit(solution)/shard_map/fit_and_apply/pallas_call | solution.py:302
  34.6 0.1 copy.16
  34.7 0.6 %copy.18 = f32[4,3,24,3]{2,0,3,1:T(4,128)} copy(f32[4,3,24,3]{2,3,1,0:T(4,128)S(1)} %bitcast.21) | data formatting | bytes 6912
  35.3 0.7 %copy.20 = f32[64,3,4,128]{3,2,1,0:T(4,128)} copy(f32[64,3,4,128]{3,2,1,0:T(4,128)S(1)} %bitcast.14) | data formatting | bytes 786432
  (4 shorter events, 0.0 us)
Async XLA Ops:
  0.6 1.3 %copy-start = (bf16[608,384]{1,0:T(8,128)(2,1)S(1)}, bf16[608,384]{1,0:T(8,128)(2,1)}, u32[]{:S(2)}) copy-start(bf16[608,384]{1,0:T(8,128)(2,1)} %constant.5.clone.table) | copy-start | bytes 1400836
  0.6 1.3 %copy-start.1 = (f32[64,3,4,128]{3,2,1,0:T(4,128)S(1)}, f32[64,3,4,128]{3,2,1,0:T(4,128)}, u32[]{:S(2)}) copy-start(f32[64,3,4,128]{3,2,1,0:T(4,128)} %param.14) | copy-start | bytes 1179652
  2.0 0.9 %copy-start.2 = (f32[16,3,4,128]{3,2,1,0:T(4,128)S(1)}, f32[16,3,4,128]{3,2,1,0:T(4,128)}, u32[]{:S(2)}) copy-start(f32[16,3,4,128]{3,2,1,0:T(4,128)} %param.8) | copy-start | bytes 294916
  2.8 0.9 %copy-start.3 = (f32[16,3,4,128]{3,2,1,0:T(4,128)S(1)}, f32[16,3,4,128]{3,2,1,0:T(4,128)}, u32[]{:S(2)}) copy-start(f32[16,3,4,128]{3,2,1,0:T(4,128)} %param.9) | copy-start | bytes 294916
  3.7 0.7 %copy-start.4 = (s32[8,4,128]{2,1,0:T(4,128)S(1)}, s32[8,4,128]{2,1,0:T(4,128)}, u32[]{:S(2)}) copy-start(s32[8,4,128]{2,1,0:T(4,128)} %param.10) | copy-start | bytes 49156
  4.5 0.7 %copy-start.5 = (s32[4,128]{1,0:T(4,128)S(1)}, s32[4,128]{1,0:T(4,128)}, u32[]{:S(2)}) copy-start(s32[4,128]{1,0:T(4,128)} %spec.1) | copy-start | bytes 6148
  5.1 0.7 %copy-start.6 = (s32[4,128]{1,0:T(4,128)S(1)}, s32[4,128]{1,0:T(4,128)}, u32[]{:S(2)}) copy-start(s32[4,128]{1,0:T(4,128)} %blk.1) | copy-start | bytes 6148

commit v2 on v1

--- a/solution.py
+++ b/solution.py
@@ -14,8 +14,9 @@
 WIDTH = 24
 PAIRS = [(p, q) for p in range(WIDTH) for q in range(p, WIDTH)]
 NPAIR = len(PAIRS)
+PLACES = {pair: index for index, pair in enumerate(PAIRS)}
 ENTRIES = 384
-PARTS = 2
+PARTS = 4
 MESH = pl.DeviceIdType.MESH
 
 offsets = ((-1, -1), (-1, 0), (-1, 1), (0, -1), (0, 1), (1, -1), (1, 0), (1, 1))
@@ -51,12 +52,21 @@
 
 def kernel(
     n_snap, n_gx, n_gy, n_dev, v_dev, scale,
-    disp, forc, neigh, spec, blk, pre, table, vec,
+    disp_in, forc_in, neigh_in, spec_in, blk_in, pre_in, table_in, vec_in,
     theta_out, out,
+    disp, forc, neigh, spec, blk, raw, table, chosen, vec, load_sem, pre, feat,
     ed, ev, ef, pk, pleft, pright, ce, pf, fleft, fright, cf,
     de, ms, prs, tall, ws, wc,
     bar_rows_s, bar_rows_r, pk_s, pk_r, t_s, t_r, f_s, f_r,
 ):
+    loads_in = [
+        pltpu.make_async_copy(source, target, load_sem.at[k])
+        for k, (source, target) in enumerate((
+            (disp_in, disp), (vec_in, vec), (neigh_in, neigh), (spec_in, spec),
+            (blk_in, blk), (forc_in, forc), (pre_in, raw), (table_in, table)))
+    ]
+    for copy in loads_in:
+        copy.start()
     me = lax.axis_index("snap")
     gx = lax.axis_index("gx")
     gy = lax.axis_index("gy")
@@ -103,10 +113,12 @@
                     send_sem=send.at[number], recv_sem=recv.at[number], device_id=(me, x, y), device_id_type=MESH))
         return made
 
-    def join_columns(from_left, from_right, target):
-        for row in range(18):
+    def join_columns(from_left, from_right, target, rows=range(18)):
+        for row in rows:
             target[row] = jnp.where(even, pltpu.roll(from_right[row], 127, 1), pltpu.roll(from_left[row], 1, 1))
 
+    loads_in[0].wait()
+    loads_in[1].wait()
     for x in range(4):
         for b in range(3):
             row = x * 3 + b
@@ -128,6 +140,8 @@
     for copy in d_rows + cols + v_rows:
         copy.start()
 
+    for copy in loads_in[2:]:
+        copy.wait()
     for o in range(8):
         for x in range(4):
             mask = neigh[pl.ds(o * 4 + x, 1), :].astype(jnp.float32)
@@ -136,6 +150,17 @@
     prs[pl.ds(372 * 8, 12 * 8), :] = jnp.zeros((12 * 8, 128), jnp.float32)
     group = blk[...] * NSPEC + spec[...]
     sub = lax.broadcasted_iota(jnp.int32, (GP * 3, 128), 0) % GP
+    n_groups = raw.shape[0] // WIDTH
+    matrices = raw[...].reshape(n_groups, WIDTH, WIDTH)
+    blank = jnp.zeros((GP - n_groups, WIDTH), jnp.float32)
+    for p in range(WIDTH):
+        held_rows = jnp.concatenate([matrices[:, p, :], blank], axis=0)
+        pre[p] = jnp.concatenate([held_rows] * 3, axis=0).T
+    chosen[...] = table[...].astype(jnp.bfloat16)
+    folds = n_dev * 4 // 8
+    for a in range(3):
+        for x in range(4):
+            feat[WIDTH + a, pl.ds(x, n_dev, stride=4), :] = forc[pl.ds(a * 4 + x, n_dev, stride=12), :]
 
     for copy in d_rows + cols:
         copy.wait_recv()
@@ -149,26 +174,24 @@
             de[1, row, pl.ds(c * 8, 8), :] = value
             de[2, row, pl.ds(c * 8, 8), :] = jnp.where(last_lane, rim, pltpu.roll(value, 127, 1))
 
+    for o, (dx, dy) in enumerate(offsets):
+        for b in range(3):
+            for x in range(4):
+                differ = de[dy + 1, (x + 1 + dx) * 3 + b] - de[1, (x + 1) * 3 + b]
+                feat[3 * o + b, pl.ds(x, n_dev, stride=4), :] = differ * ms[x, pl.ds(3 * o + b, 1), :]
+    for base in range(0, WIDTH, 4):
+        kept = [[feat[p, pl.ds(8 * k, 8), :] for k in range(folds)] for p in range(base, base + 4)]
+        for q in range(base, WIDTH + 3):
+            other = [feat[q, pl.ds(8 * k, 8), :] for k in range(folds)]
+            for p in range(base, min(base + 4, q + 1)):
+                acc = kept[p - base][0] * other[0]
+                for k in range(1, folds):
+                    acc = acc + kept[p - base][k] * other[k]
+                place = PLACES[p, q] if q < WIDTH else NPAIR + 3 * p + q - WIDTH
+                prs[pl.ds(place * 8, 8), :] = acc
     total = jnp.zeros((GP, ENTRIES), jnp.float32)
     for x in range(4):
-        feats = []
-        for o, (dx, dy) in enumerate(offsets):
-            for b in range(3):
-                differ = de[dy + 1, (x + 1 + dx) * 3 + b] - de[1, (x + 1) * 3 + b]
-                feats.append(differ * ms[x, pl.ds(3 * o + b, 1), :])
-        loads = [forc[pl.ds(a * 4 + x, n_dev, stride=12), :] for a in range(3)]
-
-        def fold(product):
-            return sum(product[c * 8:(c + 1) * 8] for c in range(d_chunks))
-
-        for index, (p, q) in enumerate(PAIRS):
-            prs[pl.ds(index * 8, 8), :] = fold(feats[p] * feats[q])
-        for p in range(WIDTH):
-            for a in range(3):
-                prs[pl.ds((NPAIR + 3 * p + a) * 8, 8), :] = fold(feats[p] * loads[a])
-        summed = prs[pl.ds(0, ENTRIES, stride=8), :]
-        for k in range(1, 8):
-            summed = summed + prs[pl.ds(k, ENTRIES, stride=8), :]
+        summed = prs[pl.ds(x, ENTRIES, stride=8), :] + prs[pl.ds(x + 4, ENTRIES, stride=8), :]
         hot = (sub[:GP] == group[x:x + 1, :]).astype(jnp.float32).astype(jnp.bfloat16)
         for piece in split(summed, 2):
             total = total + dot_nt(hot, piece)
@@ -194,14 +217,13 @@
     column = lax.broadcasted_iota(jnp.int32, (GP * 3, ENTRIES), 1)
     comp = lax.broadcasted_iota(jnp.int32, (GP * 3, ENTRIES), 0) // GP
     wide = jnp.where((column < NPAIR) | (lax.rem(column, 3) == comp), wide, 0.0)
-    full = sum(dot_nt(table[...], piece) for piece in split(wide, 3))
+    full = sum(dot_nt(chosen[...], piece) for piece in split(wide, 3))
     gram = full[: WIDTH * WIDTH].reshape(WIDTH, WIDTH, GP * 3)
     rhs = full[WIDTH * WIDTH: WIDTH * WIDTH + WIDTH]
-    inverse = pre[...].reshape(WIDTH, WIDTH, GP * 3)
+    inverse = pre[...]
     first = jnp.sum(inverse * rhs[None], axis=1)
     remain = rhs - jnp.sum(gram * first[None], axis=1)
     theta = first + jnp.sum(inverse * remain[None], axis=1)
-    theta_out[...] = theta
 
     held = lax.broadcasted_iota(jnp.int32, (WIDTH, GP * 3), 1) // GP
     stacked = jnp.concatenate([jnp.where(held == a, theta, 0.0) for a in range(3)], axis=0)
@@ -216,19 +238,19 @@
                 wc[x, pl.ds(a * 3 + b, 1), :] = jnp.sum(
                     ws[x, pl.ds(a * WIDTH + b, 8, stride=3), :], axis=0, keepdims=True)
 
-    def stencil(field, rims, chunk, index, emit):
+    def stencil(field, rims, chunk, index, emit, picked):
         start = pl.multiple_of(chunk * 8, 8)
         shift = 128 - (2 * index + 1)
-        rows = []
-        for row in range(18):
+        rows = {}
+        for row in range(picked[0] * 3, (picked[-1] + 3) * 3):
             value = field[row, pl.ds(start, 8), :]
             rim = pltpu.roll(rims[row], shift, 1)
-            rows.append((
+            rows[row] = (
                 jnp.where(first_lane, rim, pltpu.roll(value, 1, 1)),
                 value,
                 jnp.where(last_lane, rim, pltpu.roll(value, 127, 1)),
-            ))
-        for x in range(4):
+            )
+        for x in picked:
             for a in range(3):
                 acc = None
                 for b in range(3):
@@ -255,7 +277,7 @@
                 ef[row + 3, pl.ds(start, 8), :] = acc
                 pf[part, row] = pack_into(pf[part, row], acc, k)
 
-            stencil(ev, ce, chunk, chunk, emit)
+            stencil(ev, ce, chunk, chunk, emit, (0, 1, 2, 3))
             return carry
 
         lax.fori_loop(0, per, first_step, 0)
@@ -265,22 +287,37 @@
             copy.start()
         f_copies.append(columns + rows)
 
-    for part in range(PARTS):
-        for copy in f_copies[part]:
-            copy.wait_recv()
-        join_columns(fleft.at[part], fright.at[part], cf)
-
-        def second_step(k, carry, part=part):
+    turned = theta.T
+    n_blocks = theta_out.shape[2]
+    for kind in range(NSPEC):
+        for a in range(3):
+            for block in range(n_blocks):
+                row = a * GP + block * NSPEC + kind
+                theta_out[kind, a, pl.ds(block, 1), :] = turned[row:row + 1, :]
+
+    def second(part, picked):
+        def second_step(k, carry):
             chunk = part * per + k
 
             def emit(x, a, start, acc):
                 own = ev[(x + 1) * 3 + a, pl.ds(start, 8), :]
                 out[pl.ds(chunk * 96 + a * 4 + x, 8, stride=12), :] = 2.0 * acc - own
 
-            stencil(ef, cf, chunk, k, emit)
+            stencil(ef, cf.at[part], chunk, k, emit, picked)
             return carry
 
         lax.fori_loop(0, per, second_step, 0)
+
+    for part in range(PARTS):
+        f_copies[part][0].wait_recv()
+        f_copies[part][3].wait_recv()
+        join_columns(fleft.at[part], fright.at[part], cf.at[part], range(3, 15))
+        second(part, (1, 2))
+    for part in range(PARTS):
+        for k in (1, 2, 4, 5, 6, 7):
+            f_copies[part][k].wait_recv()
+        join_columns(fleft.at[part], fright.at[part], cf.at[part], (0, 1, 2, 15, 16, 17))
+        second(part, (0, 3))
 
     for copy in d_rows + cols + v_rows + t_copies + sum(f_copies, []):
         copy.wait_send()
@@ -292,22 +329,32 @@
     n_snap, n_gx, n_gy = (lax.axis_size(name) for name in ("snap", "gx", "gy"))
     n_groups = precond.shape[0] * precond.shape[1]
     scale = 1.0 / (n_dev * n_snap * AB)
-    inverse = precond.reshape(n_groups, WIDTH, WIDTH).transpose(1, 2, 0).reshape(WIDTH * WIDTH, n_groups)
-    inverse = jnp.pad(inverse, ((0, 0), (0, GP - n_groups)))
-    inverse = jnp.concatenate([inverse] * 3, axis=1)
-    table = jnp.asarray(expansion(), jnp.bfloat16)
+    table = jnp.asarray(expansion())
     vmem = pl.BlockSpec(memory_space=pltpu.VMEM)
+    hbm = pl.BlockSpec(memory_space=pltpu.HBM)
     f32 = jnp.float32
     dma = pltpu.SemaphoreType.DMA
     theta, out = pl.pallas_call(
         functools.partial(kernel, n_snap, n_gx, n_gy, n_dev, v_dev, scale),
         out_shape=(
-            jax.ShapeDtypeStruct((WIDTH, GP * 3), f32),
+            jax.ShapeDtypeStruct((NSPEC, 3, precond.shape[0], WIDTH), f32),
             jax.ShapeDtypeStruct((v_dev * 12, cols), f32),
         ),
-        in_specs=[vmem] * 8,
+        in_specs=[hbm] * 8,
         out_specs=(vmem, vmem),
         scratch_shapes=[
+            pltpu.VMEM((n_dev * 12, cols), f32),
+            pltpu.VMEM((n_dev * 12, cols), f32),
+            pltpu.VMEM((32, cols), jnp.int32),
+            pltpu.VMEM((rows, cols), jnp.int32),
+            pltpu.VMEM((rows, cols), jnp.int32),
+            pltpu.VMEM((n_groups * WIDTH, WIDTH), f32),
+            pltpu.VMEM(table.shape, f32),
+            pltpu.VMEM(table.shape, jnp.bfloat16),
+            pltpu.VMEM((v_dev * 12, cols), f32),
+            dma((8,)),
+            pltpu.VMEM((WIDTH, WIDTH, GP * 3), f32),
+            pltpu.VMEM((WIDTH + 3, n_dev * 4, cols), f32),
             pltpu.VMEM((18, n_dev, cols), f32),
             pltpu.VMEM((18, v_dev, cols), f32),
             pltpu.VMEM((18, v_dev, cols), f32),
@@ -318,7 +365,7 @@
             pltpu.VMEM((PARTS, 12, 8, cols), f32),
             pltpu.VMEM((PARTS, 18, 8, cols), f32),
             pltpu.VMEM((PARTS, 18, 8, cols), f32),
-            pltpu.VMEM((18, 8, cols), f32),
+            pltpu.VMEM((PARTS, 18, 8, cols), f32),
             pltpu.VMEM((3, 18, n_dev, cols), f32),
             pltpu.VMEM((4, WIDTH, cols), f32),
             pltpu.VMEM((ENTRIES * 8, cols), f32),
@@ -329,15 +376,14 @@
             dma((n_snap,)), dma((n_snap,)), dma((PARTS, 8)), dma((PARTS, 8)),
         ],
         compiler_params=pltpu.CompilerParams(
-            collective_id=0, has_side_effects=True, vmem_limit_bytes=40 * 1024 * 1024),
+            collective_id=0, has_side_effects=True, vmem_limit_bytes=62 * 1024 * 1024),
         name="fit_and_apply",
     )(
         displacements.reshape(n_dev * 12, cols), forces.reshape(n_dev * 12, cols),
-        neighbours.reshape(32, cols), species, block_of, inverse, table, vectors.reshape(v_dev * 12, cols),
+        neighbours.reshape(32, cols), species, block_of, precond.reshape(n_groups * WIDTH, WIDTH), table, vectors.reshape(v_dev * 12, cols),
     )
-    theta = theta.reshape(WIDTH, 3, GP)[:, :, :n_groups].transpose(2, 0, 1)
     return (
-        theta.reshape(precond.shape[0], precond.shape[1], WIDTH, 3),
+        theta.transpose(2, 0, 3, 1),
         out.reshape(v_dev, 3, rows, cols),
     )
 

time: 36.4 us -> 39.1 us (1.074)
  Pallas kernels: 28.8 us -> 35.1 us
  local copies, waits for them, and re-layouts: 6.57 us -> 3.11 us
    pallas_call x1, Pallas kernels: 28.8 us -> 35.1 us  [shards(): pl.pallas_call(functools.partial(kernel, n_snap, n_gx, n_gy, n_dev, v_dev...]
    unnamed x16 -> x2, local copies, waits for them, and re-layouts: 5.23 us -> 3.11 us
    reshape x1 -> x0, local copies, waits for them, and re-layouts: 1.09 us -> none  [shards(): precond.reshape(n_groups, WIDTH, WIDTH).transpose(1, 2, 0)]
where the time goes in v2:
time: 39.1 us; the launch traced here: 38.9 us
  Pallas kernels  35.1 us (90%)
  local copies, waits for them, and re-layouts  3.11 us (8%)
  between operations  0.64 us (2%)
    pallas_call x1, Pallas kernels, shards(): pl.pallas_call(functools.partial(kernel, n_snap, n_gx, n_gy, n_dev, v_dev...  35.1 us
    unnamed x2, local copies, waits for them, and re-layouts  3.11 us

profile of v2, /device:TPU:0, one launch (start us, length us, event | category | flops | bytes accessed | tf_op | source)
XLA Modules:
  0.0 38.9 jit_solution(8207680019206148133)
XLA Ops:
  0.6 35.1 %fit_and_apply.1 = (f32[3,3,4,24]{3,2,1,0:T(4,128)}, f32[768,128]{1,0:T(8,128)}) custom-call(f32[192,128]{1,0:T(8,128)} %bitcast.10, f32[192,128]{1,0:T(8,128)} %bitcast.11, s32[32,128]{1,0:T(8,128)} %bitcast.13, s32[4,128]{1,0:T(4,128)} %spec_in.1, s32[4,128]{1,0:T(4,128)} %blk_in.1, f32[288,24]{1,0:T(8,128)} %bitcast.9, ...), custom_call_target="tpu_custom_call" | custom-call | tf_op jit(solution)/shard_map/fit_and_apply/pallas_call | solution.py:337
  35.8 1.3 %copy.12 = f32[4,3,24,3]{2,0,3,1:T(4,128)} copy(f32[4,3,24,3]{2,0,3,1:T(4,128)} %bitcast.12) | data formatting | bytes 6912
  37.1 1.8 %copy.13 = f32[64,3,4,128]{3,2,1,0:T(4,128)} copy(f32[64,3,4,128]{3,2,1,0:T(4,128)} %bitcast.7) | data formatting | bytes 786432

commit v3 on v2

--- a/solution.py
+++ b/solution.py
@@ -12,9 +12,9 @@
 NSPEC = 3
 GP = 16
 WIDTH = 24
-PAIRS = [(p, q) for p in range(WIDTH) for q in range(p, WIDTH)]
-NPAIR = len(PAIRS)
-PLACES = {pair: index for index, pair in enumerate(PAIRS)}
+DIAGS = WIDTH // 2 + 1
+STEP = DIAGS + 3
+FORCE = WIDTH + DIAGS - 1
 ENTRIES = 384
 PARTS = 4
 MESH = pl.DeviceIdType.MESH
@@ -24,12 +24,13 @@
 
 def expansion():
     table = np.zeros((608, ENTRIES), np.float32)
-    for index, (p, q) in enumerate(PAIRS):
-        table[p * WIDTH + q, index] = 1.0
-        table[q * WIDTH + p, index] = 1.0
     for p in range(WIDTH):
-        for a in range(3):
-            table[WIDTH * WIDTH + p, NPAIR + 3 * p + a] = 1.0
+        for d in range(DIAGS):
+            q = (p + d) % WIDTH
+            table[p * WIDTH + q, p * STEP + d] = 1.0
+            if d < DIAGS - 1:
+                table[q * WIDTH + p, p * STEP + d] = 1.0
+        table[WIDTH * WIDTH + p, p * STEP + DIAGS: (p + 1) * STEP] = 1.0
     return table
 
 
@@ -54,7 +55,7 @@
     n_snap, n_gx, n_gy, n_dev, v_dev, scale,
     disp_in, forc_in, neigh_in, spec_in, blk_in, pre_in, table_in, vec_in,
     theta_out, out,
-    disp, forc, neigh, spec, blk, raw, table, chosen, vec, load_sem, pre, feat,
+    disp, forc, neigh, spec, blk, raw, table, chosen, vec, load_sem, pre, feat, grp, full, fit, half,
     ed, ev, ef, pk, pleft, pright, ce, pf, fleft, fright, cf,
     de, ms, prs, tall, ws, wc,
     bar_rows_s, bar_rows_r, pk_s, pk_r, t_s, t_r, f_s, f_r,
@@ -113,25 +114,30 @@
                     send_sem=send.at[number], recv_sem=recv.at[number], device_id=(me, x, y), device_id_type=MESH))
         return made
 
-    def join_columns(from_left, from_right, target, rows=range(18)):
-        for row in rows:
+    def join_columns(from_left, from_right, target, low=0, high=18):
+        def join(row, carry):
             target[row] = jnp.where(even, pltpu.roll(from_right[row], 127, 1), pltpu.roll(from_left[row], 1, 1))
+            return carry
+
+        lax.fori_loop(low, high, join, 0, unroll=3)
 
     loads_in[0].wait()
     loads_in[1].wait()
-    for x in range(4):
-        for b in range(3):
-            row = x * 3 + b
-            packed = jnp.zeros((8, 128), jnp.float32)
-            for c in range(d_chunks):
-                value = disp[pl.ds(c * 96 + b * 4 + x, 8, stride=12), :]
-                ed[row + 3, pl.ds(c * 8, 8), :] = value
-                packed = pack_into(packed, value, v_chunks + c)
-            for c in range(v_chunks):
-                value = vec[pl.ds(c * 96 + b * 4 + x, 8, stride=12), :]
-                ev[row + 3, pl.ds(c * 8, 8), :] = value
-                packed = pack_into(packed, value, c)
-            pk[row] = packed
+    def stage(row, carry):
+        place = lax.rem(row, 3) * 4 + row // 3
+        packed = jnp.zeros((8, 128), jnp.float32)
+        for c in range(d_chunks):
+            value = disp[pl.ds(c * 96 + place, 8, stride=12), :]
+            ed[row + 3, pl.ds(c * 8, 8), :] = value
+            packed = pack_into(packed, value, v_chunks + c)
+        for c in range(v_chunks):
+            value = vec[pl.ds(c * 96 + place, 8, stride=12), :]
+            ev[row + 3, pl.ds(c * 8, 8), :] = value
+            packed = pack_into(packed, value, c)
+        pk[row] = packed
+        return carry
+
+    lax.fori_loop(0, 12, stage, 0)
 
     pl.semaphore_wait(barrier, len(around) + len(peers))
     d_rows = row_copies(ed, pl.ds(0, n_dev), bar_rows_s.at[0], bar_rows_r.at[0])
@@ -147,26 +153,36 @@
             mask = neigh[pl.ds(o * 4 + x, 1), :].astype(jnp.float32)
             for b in range(3):
                 ms[x, pl.ds(3 * o + b, 1), :] = mask
-    prs[pl.ds(372 * 8, 12 * 8), :] = jnp.zeros((12 * 8, 128), jnp.float32)
-    group = blk[...] * NSPEC + spec[...]
+    grp[...] = blk[...] * NSPEC + spec[...]
     sub = lax.broadcasted_iota(jnp.int32, (GP * 3, 128), 0) % GP
     n_groups = raw.shape[0] // WIDTH
-    matrices = raw[...].reshape(n_groups, WIDTH, WIDTH)
     blank = jnp.zeros((GP - n_groups, WIDTH), jnp.float32)
-    for p in range(WIDTH):
-        held_rows = jnp.concatenate([matrices[:, p, :], blank], axis=0)
+
+    def turn(p, carry):
+        held_rows = jnp.concatenate([raw[pl.ds(p, n_groups, stride=WIDTH), :][:, :WIDTH], blank], axis=0)
         pre[p] = jnp.concatenate([held_rows] * 3, axis=0).T
-    chosen[...] = table[...].astype(jnp.bfloat16)
+        return carry
+
+    lax.fori_loop(0, WIDTH, turn, 0, unroll=4)
+
+    def choose(k, carry):
+        chosen[pl.ds(k * 32, 32), :] = table[pl.ds(k * 32, 32), :].astype(jnp.bfloat16)
+        return carry
+
+    lax.fori_loop(0, 19, choose, 0)
     folds = n_dev * 4 // 8
-    for a in range(3):
-        for x in range(4):
-            feat[WIDTH + a, pl.ds(x, n_dev, stride=4), :] = forc[pl.ds(a * 4 + x, n_dev, stride=12), :]
+    def place_forces(x, carry):
+        for a in range(3):
+            feat[FORCE + a, pl.ds(x, n_dev, stride=4), :] = forc[pl.ds(a * 4 + x, n_dev, stride=12), :]
+        return carry
+
+    lax.fori_loop(0, 4, place_forces, 0)
 
     for copy in d_rows + cols:
         copy.wait_recv()
     join_columns(pleft, pright, ce)
 
-    for row in range(18):
+    def widen(row, carry):
         for c in range(d_chunks):
             value = ed[row, pl.ds(c * 8, 8), :]
             rim = pltpu.roll(ce[row], 128 - (2 * (v_chunks + c) + 1), 1)
@@ -174,27 +190,43 @@
             de[1, row, pl.ds(c * 8, 8), :] = value
             de[2, row, pl.ds(c * 8, 8), :] = jnp.where(last_lane, rim, pltpu.roll(value, 127, 1))
 
-    for o, (dx, dy) in enumerate(offsets):
-        for b in range(3):
-            for x in range(4):
+        return carry
+
+    lax.fori_loop(0, 18, widen, 0)
+
+    def features(x, carry):
+        for o, (dx, dy) in enumerate(offsets):
+            for b in range(3):
+                p = 3 * o + b
                 differ = de[dy + 1, (x + 1 + dx) * 3 + b] - de[1, (x + 1) * 3 + b]
-                feat[3 * o + b, pl.ds(x, n_dev, stride=4), :] = differ * ms[x, pl.ds(3 * o + b, 1), :]
-    for base in range(0, WIDTH, 4):
-        kept = [[feat[p, pl.ds(8 * k, 8), :] for k in range(folds)] for p in range(base, base + 4)]
-        for q in range(base, WIDTH + 3):
-            other = [feat[q, pl.ds(8 * k, 8), :] for k in range(folds)]
-            for p in range(base, min(base + 4, q + 1)):
-                acc = kept[p - base][0] * other[0]
-                for k in range(1, folds):
-                    acc = acc + kept[p - base][k] * other[k]
-                place = PLACES[p, q] if q < WIDTH else NPAIR + 3 * p + q - WIDTH
-                prs[pl.ds(place * 8, 8), :] = acc
-    total = jnp.zeros((GP, ENTRIES), jnp.float32)
-    for x in range(4):
+                value = differ * ms[x, pl.ds(p, 1), :]
+                feat[p, pl.ds(x, n_dev, stride=4), :] = value
+                if p < DIAGS - 1:
+                    feat[WIDTH + p, pl.ds(x, n_dev, stride=4), :] = value
+        return carry
+
+    lax.fori_loop(0, 4, features, 0)
+
+    def products(p, carry):
+        kept = [feat[p, pl.ds(8 * k, 8), :] for k in range(folds)]
+        for d in range(STEP):
+            q = p + d if d < DIAGS else FORCE + d - DIAGS
+            acc = kept[0] * feat[q, pl.ds(0, 8), :]
+            for k in range(1, folds):
+                acc = acc + kept[k] * feat[q, pl.ds(8 * k, 8), :]
+            prs[pl.ds(pl.multiple_of((p * STEP + d) * 8, 8), 8), :] = acc
+        return carry
+
+    lax.fori_loop(0, WIDTH, products, 0)
+
+    def regroup(x, total):
         summed = prs[pl.ds(x, ENTRIES, stride=8), :] + prs[pl.ds(x + 4, ENTRIES, stride=8), :]
-        hot = (sub[:GP] == group[x:x + 1, :]).astype(jnp.float32).astype(jnp.bfloat16)
+        hot = (sub[:GP] == grp[pl.ds(x, 1), :]).astype(jnp.float32).astype(jnp.bfloat16)
         for piece in split(summed, 2):
             total = total + dot_nt(hot, piece)
+        return total
+
+    total = lax.fori_loop(0, 4, regroup, jnp.zeros((GP, ENTRIES), jnp.float32))
 
     tall[me] = total
     t_copies = []
@@ -216,20 +248,31 @@
     wide = jnp.concatenate([total, total, total], axis=0)
     column = lax.broadcasted_iota(jnp.int32, (GP * 3, ENTRIES), 1)
     comp = lax.broadcasted_iota(jnp.int32, (GP * 3, ENTRIES), 0) // GP
-    wide = jnp.where((column < NPAIR) | (lax.rem(column, 3) == comp), wide, 0.0)
-    full = sum(dot_nt(chosen[...], piece) for piece in split(wide, 3))
-    gram = full[: WIDTH * WIDTH].reshape(WIDTH, WIDTH, GP * 3)
-    rhs = full[WIDTH * WIDTH: WIDTH * WIDTH + WIDTH]
-    inverse = pre[...]
-    first = jnp.sum(inverse * rhs[None], axis=1)
-    remain = rhs - jnp.sum(gram * first[None], axis=1)
-    theta = first + jnp.sum(inverse * remain[None], axis=1)
+    kind_of = column % STEP
+    wide = jnp.where((kind_of < DIAGS) | (kind_of - DIAGS == comp), wide, 0.0)
+    wide_pieces = split(wide, 3)
+    for block in range(2):
+        part_of = pl.ds(block * 304, 304)
+        full[part_of, :] = sum(dot_nt(chosen[part_of, :], piece) for piece in wide_pieces)
+    rhs = full[pl.ds(WIDTH * WIDTH, WIDTH), :]
+
+    def apply_to(rows_of, operand, target):
+        def one(p, carry):
+            target[pl.ds(p, 1), :] = jnp.sum(rows_of(p) * operand, axis=0, keepdims=True)
+            return carry
+
+        lax.fori_loop(0, WIDTH, one, 0, unroll=8)
+        return target[...]
+
+    first = apply_to(lambda p: pre[p], rhs, fit)
+    remain = rhs - apply_to(lambda p: full[pl.ds(pl.multiple_of(p * WIDTH, 8), WIDTH), :], first, half)
+    theta = first + apply_to(lambda p: pre[p], remain, fit)
 
     held = lax.broadcasted_iota(jnp.int32, (WIDTH, GP * 3), 1) // GP
     stacked = jnp.concatenate([jnp.where(held == a, theta, 0.0) for a in range(3)], axis=0)
     pieces = split(stacked, 3)
-    for x in range(4):
-        hot = (sub == group[x:x + 1, :]).astype(jnp.float32).astype(jnp.bfloat16)
+    def weigh(x, carry):
+        hot = (sub == grp[pl.ds(x, 1), :]).astype(jnp.float32).astype(jnp.bfloat16)
         values = sum(dot_nn(piece, hot) for piece in pieces)
         mask = ms[x]
         ws[x] = values * jnp.concatenate([mask, mask, mask], axis=0)
@@ -237,6 +280,9 @@
             for b in range(3):
                 wc[x, pl.ds(a * 3 + b, 1), :] = jnp.sum(
                     ws[x, pl.ds(a * WIDTH + b, 8, stride=3), :], axis=0, keepdims=True)
+        return carry
+
+    lax.fori_loop(0, 4, weigh, 0)
 
     def stencil(field, rims, chunk, index, emit, picked):
         start = pl.multiple_of(chunk * 8, 8)
@@ -265,11 +311,15 @@
         copy.wait_recv()
 
     per = v_chunks // PARTS
-    f_copies = []
-    for part in range(PARTS):
-        pf[part] = jnp.zeros((12, 8, 128), jnp.float32)
-
-        def first_step(k, carry, part=part):
+    pf[...] = jnp.zeros(pf.shape, jnp.float32)
+
+    def sent(part):
+        rows = row_copies(ef, pl.ds(pl.multiple_of(part * (per * 8), 8), per * 8), f_s.at[part], f_r.at[part])
+        columns = column_copies(pf.at[part], fleft.at[part], fright.at[part], f_s.at[part], f_r.at[part], 2)
+        return columns + rows
+
+    def first_part(part, carry):
+        def first_step(k, carry):
             chunk = part * per + k
 
             def emit(x, a, start, acc):
@@ -281,11 +331,11 @@
             return carry
 
         lax.fori_loop(0, per, first_step, 0)
-        rows = row_copies(ef, pl.ds(part * per * 8, per * 8), f_s.at[part], f_r.at[part])
-        columns = column_copies(pf.at[part], fleft.at[part], fright.at[part], f_s.at[part], f_r.at[part], 2)
-        for copy in columns + rows:
+        for copy in sent(part):
             copy.start()
-        f_copies.append(columns + rows)
+        return carry
+
+    lax.fori_loop(0, PARTS, first_part, 0)
 
     turned = theta.T
     n_blocks = theta_out.shape[2]
@@ -308,18 +358,28 @@
 
         lax.fori_loop(0, per, second_step, 0)
 
-    for part in range(PARTS):
-        f_copies[part][0].wait_recv()
-        f_copies[part][3].wait_recv()
-        join_columns(fleft.at[part], fright.at[part], cf.at[part], range(3, 15))
+    def inner(part, carry):
+        copies = sent(part)
+        copies[0].wait_recv()
+        copies[3].wait_recv()
+        join_columns(fleft.at[part], fright.at[part], cf.at[part], 3, 15)
         second(part, (1, 2))
-    for part in range(PARTS):
+        return carry
+
+    def outer(part, carry):
+        copies = sent(part)
         for k in (1, 2, 4, 5, 6, 7):
-            f_copies[part][k].wait_recv()
-        join_columns(fleft.at[part], fright.at[part], cf.at[part], (0, 1, 2, 15, 16, 17))
+            copies[k].wait_recv()
+        join_columns(fleft.at[part], fright.at[part], cf.at[part], 0, 3)
+        join_columns(fleft.at[part], fright.at[part], cf.at[part], 15, 18)
         second(part, (0, 3))
-
-    for copy in d_rows + cols + v_rows + t_copies + sum(f_copies, []):
+        for copy in copies:
+            copy.wait_send()
+        return carry
+
+    lax.fori_loop(0, PARTS, inner, 0)
+    lax.fori_loop(0, PARTS, outer, 0)
+    for copy in d_rows + cols + v_rows + t_copies:
         copy.wait_send()
 
 
@@ -354,7 +414,11 @@
             pltpu.VMEM((v_dev * 12, cols), f32),
             dma((8,)),
             pltpu.VMEM((WIDTH, WIDTH, GP * 3), f32),
-            pltpu.VMEM((WIDTH + 3, n_dev * 4, cols), f32),
+            pltpu.VMEM((FORCE + 3, n_dev * 4, cols), f32),
+            pltpu.VMEM((4, cols), jnp.int32),
+            pltpu.VMEM((608, GP * 3), f32),
+            pltpu.VMEM((WIDTH, GP * 3), f32),
+            pltpu.VMEM((WIDTH, GP * 3), f32),
             pltpu.VMEM((18, n_dev, cols), f32),
             pltpu.VMEM((18, v_dev, cols), f32),
             pltpu.VMEM((18, v_dev, cols), f32),

time: 39.1 us -> 42.4 us (1.084)
  Pallas kernels: 35.1 us -> 38.5 us
    pallas_call x1, Pallas kernels: 35.1 us -> 38.5 us  [shards(): pl.pallas_call(functools.partial(kernel, n_snap, n_gx, n_gy, n_dev, v_dev...]
where the time goes in v3:
time: 42.4 us; the launch traced here: 42.2 us
  Pallas kernels  38.5 us (91%)
  local copies, waits for them, and re-layouts  3.11 us (7%)
  between operations  0.64 us (2%)
    pallas_call x1, Pallas kernels, shards(): pl.pallas_call(functools.partial(kernel, n_snap, n_gx, n_gy, n_dev, v_dev...  38.5 us
    unnamed x2, local copies, waits for them, and re-layouts  3.11 us

profile of v3, /device:TPU:0, one launch (start us, length us, event | category | flops | bytes accessed | tf_op | source)
XLA Modules:
  0.0 42.2 jit_solution(7046325335739546618)
XLA Ops:
  0.6 38.5 %fit_and_apply.1 = (f32[3,3,4,24]{3,2,1,0:T(4,128)}, f32[768,128]{1,0:T(8,128)}) custom-call(f32[192,128]{1,0:T(8,128)} %bitcast.10, f32[192,128]{1,0:T(8,128)} %bitcast.11, s32[32,128]{1,0:T(8,128)} %bitcast.13, s32[4,128]{1,0:T(4,128)} %spec_in.1, s32[4,128]{1,0:T(4,128)} %blk_in.1, f32[288,24]{1,0:T(8,128)} %bitcast.9, ...), custom_call_target="tpu_custom_call" | custom-call | tf_op jit(solution)/shard_map/fit_and_apply/pallas_call | solution.py:397
  39.1 1.3 %copy.12 = f32[4,3,24,3]{2,0,3,1:T(4,128)} copy(f32[4,3,24,3]{2,0,3,1:T(4,128)} %bitcast.12) | data formatting | bytes 6912
  40.4 1.8 %copy.13 = f32[64,3,4,128]{3,2,1,0:T(4,128)} copy(f32[64,3,4,128]{3,2,1,0:T(4,128)} %bitcast.7) | data formatting | bytes 786432
